TPU v7x, 512 devices: a whole 4x4x16 slice. The times are simulated.
512 devices in a mesh: seq: 64 (over x, z), exp: 8 (over y, core).
Axes of the slice: x: 4, y: 4, z: 16, core: 2. Of those that a mesh axis runs over, the one named last changes fastest.
Arguments:
- queries: bfloat16 [4096, 6144], P('seq', 'exp'), may hold values from -6 to 6
- keys: bfloat16 [4096, 6144], P('seq', 'exp'), may hold values from -6 to 6
- values: bfloat16 [4096, 6144], P('seq', 'exp'), may hold values from -6 to 6
- log_decay: float32 [48, 4096], P('exp', 'seq'), may hold values from -1 to 0
- state_in: float32 [48, 128, 128], P('exp'), may hold values from -24 to 24
- norm_gain: float32 [6144], replicated, may hold values from 0.1 to 1.9
- routes: int32 [4096, 2], P('seq'), may hold values from 0 to 7, all different within a row; in each aligned block of 64 rows (0 to 63, 64 to 127, ...) at most 20 rows name the same one
- w_gate: bfloat16 [8, 9216, 6144], P('exp', 'seq'), may hold values from -0.078125 to 0.078125
- w_up: bfloat16 [8, 9216, 6144], P('exp', 'seq'), may hold values from -0.078125 to 0.078125
Outputs:
- expert_hidden: bfloat16 [8, 9216, 1280], P('exp', 'seq')
- state_out: float32 [48, 128, 128], P('exp', 'seq')
Inputs may be any that keep to these rules, and one draw needn't show every extreme that they name: `routes`: each token names two different experts; in each aligned block of 64 tokens no expert is named by more than 20 tokens, and some blocks reach exactly 20.
All inputs are finite; a program needn't handle non-finite values.
Results may differ from a plain program's by a relative error of at most 0.0071.
Values may be sent and summed in bfloat16 or wider, within the bound.
A program may use at most 128 MiB of HBM per device.

v0:
```python
import math

import jax
import jax.numpy as jnp
from jax import lax
from jax.sharding import PartitionSpec as P

CAP = 20


epsilon = 1e-06


def prefix(part, axis, combine, identity):
    place = lax.axis_index(axis)
    gathered = jax.tree.map(lambda a: lax.all_gather(a, axis), part)
    state = jax.tree.map(lambda a, e: jnp.zeros_like(a) + jnp.asarray(e, a.dtype), part, identity)

    def one(hop, state):
        return combine(
            state, jax.tree.map(lambda a: lax.dynamic_index_in_dim(a, hop, 0, False), gathered)
        )

    return lax.fori_loop(0, place, one, state)


def compose(earlier, later_pair):
    return (
        earlier[0] + later_pair[0],
        jnp.exp(later_pair[0])[:, None, None] * earlier[1] + later_pair[1],
    )


def select_rows(routes, expert_ids, capacity, source):
    chosen = jnp.any(routes[None, :, :] == expert_ids[:, None, None], axis=2).astype(jnp.int32)
    position = jnp.cumsum(chosen, axis=1) - 1
    slot_ids = jnp.arange(capacity, dtype=jnp.int32)
    selector = (
        (chosen[:, None, :] == 1) & (position[:, None, :] == slot_ids[None, :, None])
    ).astype(jnp.bfloat16)
    return jnp.einsum("nct,tf->ncf", selector, source, preferred_element_type=jnp.float32).astype(
        jnp.bfloat16
    )


def shards(queries, keys, values, log_decay, state_in, norm_gain, routes, w_gate, w_up):
    length = queries.shape[0]
    features = queries.shape[1]
    local_heads = state_in.shape[0]
    head_dim = state_in.shape[1]
    scaling = 1.0 / math.sqrt(head_dim)
    query_blk = queries.reshape(length, local_heads, head_dim)
    key_blk = keys.reshape(length, local_heads, head_dim)
    value_blk = values.reshape(length, local_heads, head_dim)
    cumlog = jnp.cumsum(log_decay, axis=1)
    block_log = cumlog[:, -1]
    causal = jnp.arange(length)[:, None] >= jnp.arange(length)[None, :]
    scores = (
        jnp.einsum("ihd,jhd->hij", query_blk, key_blk, preferred_element_type=jnp.float32) * scaling
    )
    gap_log = cumlog[:, :, None] - cumlog[:, None, :]
    weights = jnp.where(causal[None], jnp.exp(jnp.where(causal[None], gap_log, 0.0)), 0.0)
    decayed = (scores * weights).astype(jnp.bfloat16)
    inside = jnp.einsum("hij,jhd->ihd", decayed, value_blk, preferred_element_type=jnp.float32)
    key_weighted = key_blk.astype(jnp.float32) * jnp.exp(block_log[:, None] - cumlog).T[:, :, None]
    block_state = jnp.einsum(
        "jhd,jhe->hde", key_weighted, value_blk.astype(jnp.float32), precision=lax.Precision.HIGHEST
    )
    before_log, before_state = prefix(
        (block_log, block_state),
        "seq",
        compose,
        (jnp.zeros_like(block_log), jnp.zeros_like(block_state)),
    )
    entering = jnp.exp(before_log)[:, None, None] * state_in + before_state
    carried_in = jnp.einsum(
        "ihd,hde->ihe",
        query_blk.astype(jnp.float32) * scaling,
        entering,
        precision=lax.Precision.HIGHEST,
    )
    carried_in = carried_in * jnp.exp(cumlog).T[:, :, None]
    attended = (inside + carried_in).astype(jnp.bfloat16).reshape(length, features)
    chain_log = lax.psum(block_log, "seq")
    later_log = chain_log - before_log - block_log
    weighted = jnp.exp(later_log)[:, None, None] * block_state
    reduced = lax.psum_scatter(weighted, "seq", scatter_dimension=1, tiled=True)
    row_count = reduced.shape[1]
    carried_rows = lax.dynamic_slice_in_dim(
        state_in, lax.axis_index("seq") * row_count, row_count, 1
    )
    state_out = reduced + jnp.exp(chain_log)[:, None, None] * carried_rows
    local_experts = w_gate.shape[0]
    gathered = lax.all_gather(attended, "exp", axis=1, tiled=True)
    expert_ids = lax.axis_index("exp") * local_experts + jnp.arange(local_experts, dtype=jnp.int32)
    row_set = select_rows(routes, expert_ids, CAP, gathered)
    row_wide = row_set.astype(jnp.float32)
    normed = (
        row_wide
        * lax.rsqrt(jnp.mean(row_wide * row_wide, axis=2, keepdims=True) + epsilon)
        * norm_gain
    ).astype(jnp.bfloat16)
    block_part = lax.all_gather(normed, "seq", axis=1, tiled=True)
    gate_act = jnp.einsum("efd,end->efn", w_gate, block_part, preferred_element_type=jnp.float32)
    up_act = jnp.einsum("efd,end->efn", w_up, block_part, preferred_element_type=jnp.float32)
    expert_hidden = (jax.nn.silu(gate_act) * up_act).astype(jnp.bfloat16)
    return (expert_hidden, state_out)


def solution(mesh):
    placed = (
        P("seq", "exp"),
        P("seq", "exp"),
        P("seq", "exp"),
        P("exp", "seq"),
        P("exp", None, None),
        P(),
        P("seq", None),
        P("exp", "seq", None),
        P("exp", "seq", None),
    )
    return jax.shard_map(
        shards,
        mesh=mesh,
        in_specs=placed,
        out_specs=(P("exp", "seq", None), P("exp", "seq", None)),
        check_vma=False,
    )
```

profile of v0, /device:TPU:1, one launch (start us, length us, event | category | flops | bytes accessed | tf_op | source)
XLA Modules:
  0.0 845.0 jit_solution(10170178238828046064)
XLA Ops:
  7.2 0.0 all-gather.7.cloned.1.call-start
  7.2 1.0 reduce_window_sum.18
  8.2 0.2 slice_reduce_fusion
  8.4 0.1 exponential_bitcast_fusion
  8.5 0.1 copy.27
  8.6 1.0 reshape.163
  9.6 0.1 convert_multiply_fusion.1
  9.8 2.2 fusion.16
  12.0 0.0 all-reduce.5.cloned.1.call-start
  12.0 1.4 fusion.46
  14.1 0.2 dynamic-update-slice
  14.3 123.5 %all-reduce.2 = (f32[384]{0:T(512)S(1)}, f32[6]{0:T(128)S(1)}) all-reduce(f32[384]{0:T(512)S(1)} %dynamic-update-slice, f32[6]{0:T(128)S(1)} %slice_reduce_fusion), channel_id=2, replica_groups=mesh['seq'=64,'exp'=8] {'seq'}, use_global_device_ids=true, to_apply=%add | all-reduce | flops 390 | bytes 3120
  137.8 0.1 reshape.170
  137.9 0.7 compare_reduce_fusion
  138.6 0.1 copy.23
  138.7 0.1 reduce-window.7
  138.8 1.0 reshape.162
  139.9 0.1 add_reduce_fusion
  140.0 1.3 convolution_bitcast_fusion.3
  141.3 120.3 %all-gather.7.cloned.1.call-done = f32[384,128,128]{2,1,0:T(8,128)} async-done(((f32[6,128,128]{2,1,0:T(8,128)}), f32[384,128,128]{2,1,0:T(8,128)}) %all-gather.7.cloned.1.call-update) | async-done | bytes 25165840 | tf_op jit(solution)/shard_map/all_gather | solution.py:16
  261.7 1.6 fusion.11
  263.3 1.9 broadcast_multiply_fusion
  265.2 0.0 all-gather.9.cloned.1.call-start
  265.3 14.6 %all_gather.18 = bf16[64,6144]{1,0:T(8,128)(2,1)S(1)} all-gather(bf16[64,768]{1,0:T(8,128)(2,1)S(1)} %bitcast.90), channel_id=1, replica_groups=mesh['seq'=64,'exp'=8] {'exp'}, dimensions={1}, use_global_device_ids=true | all-gather | bytes 884736 | tf_op jit(solution)/shard_map/all_gather | solution.py:94
  279.9 0.3 multiply_reduce_fusion
  280.3 1.6 fusion.14
  282.5 301.2 %all-reduce.5.cloned.1.call-done = f32[6,128,128]{2,1,0:T(8,128)} async-done(((f32[6,128,128]{2,1,0:T(8,128)}), f32[6,128,128]{2,1,0:T(8,128)}) %all-reduce.5.cloned.1.call-update) | async-done | bytes 393232
  583.8 1.4 dynamic-slice_add_fusion
  585.2 212.3 %all-gather.9.cloned.1.call-done = bf16[64,20,6144]{2,1,0:T(8,128)(2,1)} async-done(((bf16[1,20,6144]{2,1,0:T(8,128)(2,1)}), bf16[64,20,6144]{2,1,0:T(8,128)(2,1)}) %all-gather.9.cloned.1.call-update) | async-done | bytes 15728656 | tf_op jit(solution)/shard_map/all_gather | solution.py:103
  797.5 23.9 %reshape.178 = bf16[1280,6144]{1,0:T(8,128)(2,1)} reshape(bf16[64,20,6144]{2,1,0:T(8,128)(2,1)} %all-gather.9.cloned.1.call-done) | data formatting | bytes 31457280
  821.4 11.0 %convolution_bitcast_fusion.1 = f32[144,1280]{1,0:T(8,128)S(1)} fusion(bf16[1280,6144]{1,0:T(8,128)(2,1)} %reshape.178, bf16[1,144,6144]{2,1,0:T(8,128)(2,1)S(1)} %copy-done), kind=kOutput, calls=%fused_computation.8 | convolution fusion | flops 2264924160 | bytes 18235392 | tf_op jit(solution)/shard_map/efd,end->efn/dot_general | solution.py:104
  832.4 6.1 fusion.3
  (19 shorter events, 0.2 us)
Async XLA Ops:
  7.2 814.2 %copy-start = (bf16[1,144,6144]{2,1,0:T(8,128)(2,1)S(1)}, bf16[1,144,6144]{2,1,0:T(8,128)(2,1)}, u32[]{:S(2)}) copy-start(bf16[1,144,6144]{2,1,0:T(8,128)(2,1)} %param.18) | copy-start | bytes 5308420
  7.2 254.5 %all-gather.7.cloned.1.call-start = ((), (), s32[]{:S(2)}) async-start(), calls=%async_computation | async-start | bytes 25559040 | tf_op jit(solution)/shard_map/all_gather | solution.py:16
  12.0 571.8 %all-reduce.5.cloned.1.call-start = ((), (), s32[]{:S(2)}) async-start(), calls=%async_computation.2 | async-start | bytes 786432
  265.2 532.3 %all-gather.9.cloned.1.call-start = ((), (), s32[]{:S(2)}) async-start(), calls=%async_computation.1 | async-start | bytes 19169280 | tf_op jit(solution)/shard_map/all_gather | solution.py:103
  821.4 11.0 %copy-start.1 = (bf16[1280,6144]{1,0:T(8,128)(2,1)S(1)}, bf16[1280,6144]{1,0:T(8,128)(2,1)}, u32[]{:S(2)}) copy-start(bf16[1280,6144]{1,0:T(8,128)(2,1)} %reshape.178) | copy-start | bytes 47185924
  821.4 11.0 %copy-start.2 = (bf16[1,144,6144]{2,1,0:T(8,128)(2,1)S(1)}, bf16[1,144,6144]{2,1,0:T(8,128)(2,1)}, u32[]{:S(2)}) copy-start(bf16[1,144,6144]{2,1,0:T(8,128)(2,1)} %param.19) | copy-start | bytes 5308420
Sparse Core Ops, SparseCore 0:
  12.1 249.5 all-gather.6
  265.3 318.3 all-reduce.4
  587.3 210.1 all-gather.8
where the time goes:
time: 849 us; the launch traced here: 845 us
  waiting for transfers between devices  634 us (75%)
  blocking collectives  138 us (16%)
  local copies, waits for them, and re-layouts  28.1 us (3%)
  matrix products  22.5 us (3%)
  between operations  15.2 us (2%)
    unnamed x4, waiting for transfers between devices  301 us
    all_gather x1, waiting for transfers between devices, shards(): block_part = lax.all_gather(normed, 'seq', axis=1, tiled=True)  212 us
    unnamed x1, blocking collectives  123 us
    all_gather x1, waiting for transfers between devices, prefix(): gathered = jax.tree.map(lambda a: lax.all_gather(a, axis), part)  120 us
    unnamed x10, local copies, waits for them, and re-layouts  25.5 us
  transfers between devices with their start and end apart: 3, of which 3 were waited for; matrix products, arithmetic and copies ran while one was open for 1% of the time, Pallas kernels for 0%

commit v1 on v0

v1 whole, which is shorter than its diff:
```python
import functools
import math

import jax
import jax.numpy as jnp
from jax import lax
from jax.experimental import pallas as pl
from jax.experimental.pallas import tpu as pltpu
from jax.sharding import PartitionSpec as P

MESH = pl.DeviceIdType.MESH
CAP = 20
EPSILON = 1e-06
NX = 4
HIGHEST = lax.Precision.HIGHEST
F32, BF16 = jnp.float32, jnp.bfloat16


def iota(shape, dim):
    return lax.broadcasted_iota(jnp.int32, shape, dim)


def dot(a, b, dims=((1,), (0,)), precision=None):
    return lax.dot_general(a, b, (dims, ((), ())), precision=precision, preferred_element_type=F32)


def remote(src, dst, send, recv, where):
    return pltpu.make_async_remote_copy(
        src_ref=src, dst_ref=dst, send_sem=send, recv_sem=recv, device_id=where, device_id_type=MESH
    )


def enter(peers):
    barrier = pltpu.get_barrier_semaphore()
    for peer in peers:
        pl.semaphore_signal(barrier, inc=1, device_id=peer, device_id_type=MESH)
    pl.semaphore_wait(barrier, len(peers))


def attend_kernel(
    nz, ne, q_ref, k_ref, v_ref, ld_ref, sin_ref, routes_ref, gain_ref, gain4_ref,
    unit_ref, sout_ref,
    stage, send1, recv1, xbuf, send2, recv2, ent, att, sende, recve,
    s1, r1, sx_sem, rx_sem, s2, r2, se, re,
):
    tokens = q_ref.shape[0]
    heads = ld_ref.shape[0]
    hd = sin_ref.shape[1]
    rows = hd // nz
    part = rows // NX
    width = heads * hd
    scaling = 1.0 / math.sqrt(hd)
    place = lax.axis_index("seq")
    x, z = place // nz, place % nz
    me = lax.axis_index("exp")
    zpeers = [(j, lax.rem(z + j, nz)) for j in range(1, nz)]
    xpeers = [(j, lax.rem(x + j, NX)) for j in range(1, NX)]
    epeers = [(j, lax.rem(me + j, ne)) for j in range(1, ne)]
    enter(
        [{"seq": x * nz + p} for _, p in zpeers]
        + [{"seq": p * nz + z} for _, p in xpeers]
        + [{"exp": p} for _, p in epeers]
    )

    ld = ld_ref[...]
    at_or_before = (iota((tokens, tokens), 0) <= iota((tokens, tokens), 1)).astype(F32)
    causal = iota((tokens, tokens), 0) >= iota((tokens, tokens), 1)
    cum = dot(ld, at_or_before, precision=HIGHEST)
    cumt = dot(causal.astype(F32), ld, ((1,), (1,)), HIGHEST)

    d = iota((hd, hd), 0)
    per_x = hd // NX
    order = (d % per_x) // part * rows + d // per_x * part + d % part
    perm = (order == iota((hd, hd), 1)).astype(BF16)

    def cols(h):
        return slice(h * hd, (h + 1) * hd)

    qs, ks = [], []
    for h in range(heads):
        qs.append(dot(q_ref[:, cols(h)], perm).astype(BF16))
        ks.append(dot(k_ref[:, cols(h)], perm).astype(BF16))
    for h in range(heads):
        last = cum[h : h + 1, tokens - 1 : tokens]
        kw = ks[h].astype(F32) * jnp.exp(last - cumt[:, h : h + 1])
        high = kw.astype(BF16)
        low = (kw - high.astype(F32)).astype(BF16)
        vh = v_ref[:, cols(h)]
        state = dot(high, vh, ((0,), (0,))) + dot(low, vh, ((0,), (0,)))
        stage[:, h * rows : (h + 1) * rows, :] = state.reshape(nz, rows, hd)
    srows = heads * rows
    send1[:, 0:srows, :] = stage[...].astype(BF16)
    total = jnp.broadcast_to(cum[:, tokens - 1 : tokens], (heads, hd))
    total = jnp.concatenate([total, jnp.zeros((8 - heads, hd), F32)], axis=0)
    high = total.astype(BF16).astype(F32)
    logs = jnp.concatenate([high, total - high], axis=0).astype(BF16)
    send1[:, srows : srows + 16, :] = jnp.broadcast_to(logs[None], (nz, 16, hd))

    firsts = []
    for j, p in zpeers:
        c = remote(send1.at[p], recv1.at[z], s1.at[j], r1.at[j], {"seq": x * nz + p})
        c.start()
        firsts.append(c)
    recv1[z] = send1[z]

    for h in range(heads):
        scores = dot(qs[h], ks[h], ((1,), (1,))) * scaling
        gap = cumt[:, h : h + 1] - cum[h : h + 1, :]
        weights = jnp.where(causal, jnp.exp(jnp.where(causal, gap, 0.0)), 0.0)
        att[:, cols(h)] = dot((scores * weights).astype(BF16), v_ref[:, cols(h)])

    group = me // (ne // 4)
    expert = iota((ne, tokens), 0)
    chosen = (routes_ref[0:1, :] == expert) | (routes_ref[1:2, :] == expert)
    position = dot(chosen.astype(F32), at_or_before, precision=HIGHEST) - 1.0
    position = jnp.where(chosen, position, -1.0)
    line = iota((32, tokens), 0)
    slot = jnp.where(line < 16, line, jnp.where((line - 16) // 4 == group, 16 + line % 4, -5))
    slot = slot.astype(F32)
    selector = jnp.concatenate(
        [
            (jnp.abs(slot - position[e : e + 1, :]) < 0.5).astype(F32).astype(BF16)
            for e in range(ne)
        ],
        axis=0,
    )

    for j, p in zpeers:
        src = lax.rem(z + nz - j, nz)
        remote(send1.at[src], recv1.at[src], s1.at[j], r1.at[j], {"seq": x * nz + src}).wait_recv()

    def block(j):
        piece = recv1[j].astype(F32)
        logs = piece[srows : srows + 8] + piece[srows + 8 : srows + 16]
        return piece, logs

    def step(running, piece, decay):
        return [
            decay[h : h + 1, :] * running[h] + piece[h * rows : (h + 1) * rows]
            for h in range(heads)
        ]

    running = [jnp.zeros((rows, hd), F32)] * heads
    whole = jnp.zeros((8, hd), F32)
    for j in range(nz):
        piece, logs = block(j)
        running = step(running, piece, jnp.exp(logs))
        whole = whole + logs
    for h in range(heads):
        xbuf[x, h * rows : (h + 1) * rows, :] = running[h]
    xbuf[x, srows : srows + 8, :] = whole
    seconds = []
    for j, p in xpeers:
        c = remote(xbuf.at[x], xbuf.at[x], sx_sem.at[j], rx_sem.at[j], {"seq": p * nz + z})
        c.start()
        seconds.append(c)
    for j, p in xpeers:
        src = lax.rem(x + NX - j, NX)
        remote(
            xbuf.at[src], xbuf.at[src], sx_sem.at[j], rx_sem.at[j], {"seq": src * nz + z}
        ).wait_recv()

    final = [sin_ref[h * rows : (h + 1) * rows, :] for h in range(heads)]
    entering = final
    for g in range(NX):
        entering = [jnp.where(x == g, f, e) for f, e in zip(final, entering)]
        final = step(final, xbuf[g], jnp.exp(xbuf[g, srows : srows + 8, :]))
    for j in range(nz):
        send2[j] = jnp.concatenate(entering, axis=0).astype(BF16)
        if j < nz - 1:
            piece, logs = block(j)
            entering = step(entering, piece, jnp.exp(logs))
    thirds = []
    for j, p in zpeers:
        c = remote(send2.at[p], recv2.at[z], s2.at[j], r2.at[j], {"seq": x * nz + p})
        c.start()
        thirds.append(c)
    recv2[z] = send2[z]
    for h in range(heads):
        mine = jnp.zeros((part, hd), F32)
        for g in range(NX):
            mine = jnp.where(x == g, final[h][g * part : (g + 1) * part], mine)
        sout_ref[h] = mine
    for j, p in zpeers:
        src = lax.rem(z + nz - j, nz)
        remote(send2.at[src], recv2.at[src], s2.at[j], r2.at[j], {"seq": x * nz + src}).wait_recv()

    ent[...] = recv2[...].astype(F32)
    parts = []
    for h in range(heads):
        state = ent[:, h * rows : (h + 1) * rows, :].reshape(hd, hd).astype(BF16)
        carried = dot(qs[h], state) * scaling * jnp.exp(cumt[:, h : h + 1])
        parts.append((att[:, cols(h)] + carried).astype(BF16))
    attended = jnp.concatenate(parts, axis=1)
    for e in range(ne):
        sende[e] = dot(selector[e * 32 : (e + 1) * 32], attended).astype(BF16)
    fourths = []
    for j, p in epeers:
        c = remote(sende.at[p], recve.at[me], se.at[j], re.at[j], {"exp": p})
        c.start()
        fourths.append(c)
    recve[me] = sende[me]
    for j, p in epeers:
        src = lax.rem(me + ne - j, ne)
        remote(sende.at[src], recve.at[src], se.at[j], re.at[j], {"exp": src}).wait_recv()

    depth = ne * width
    wide = [recve[e].astype(F32) for e in range(ne)]
    main = [w[0:16] for w in wide]
    halves = ne // 4
    rest = [sum(wide[g * halves + i][16:32] for g in range(4)) for i in range(halves)]
    square = sum(jnp.sum(m * m, axis=1, keepdims=True) for m in main)
    scale = lax.rsqrt(square / depth + EPSILON)
    for e in range(ne):
        at = slice(e * width, (e + 1) * width)
        unit_ref[:, at] = (main[e] * scale * gain_ref[:, at]).astype(BF16)
    square = sum(jnp.sum(m * m, axis=1, keepdims=True) for m in rest)
    same = (iota((16, 16), 0) % 4 == iota((16, 16), 1) % 4).astype(F32)
    square = dot(same, jnp.broadcast_to(square, (16, 128)), precision=HIGHEST)[:, 0:1]
    scale = lax.rsqrt(square / depth + EPSILON)
    for i in range(halves):
        at = slice(i * width, (i + 1) * width)
        unit_ref[:, depth + i * width : depth + (i + 1) * width] = (
            rest[i] * scale * gain4_ref[:, at]
        ).astype(BF16)

    for c in firsts + seconds + thirds + fourths:
        c.wait_send()


def attend(nz, ne, q, k, v, ld, sin, routes, gain, gain4):
    tokens, width = q.shape
    heads, hd = ld.shape[0], sin.shape[1]
    rows = hd // nz
    depth = ne * width
    dma = pltpu.SemaphoreType.DMA
    vmem = pl.BlockSpec(memory_space=pltpu.VMEM)
    return pl.pallas_call(
        functools.partial(attend_kernel, nz, ne),
        out_shape=(
            jax.ShapeDtypeStruct((16, depth + depth // 4), BF16),
            jax.ShapeDtypeStruct((heads, rows // NX, hd), F32),
        ),
        in_specs=[vmem] * 8,
        out_specs=(vmem, vmem),
        scratch_shapes=[
            pltpu.VMEM((nz, heads * rows, hd), F32),
            pltpu.VMEM((nz, heads * rows + 16, hd), BF16),
            pltpu.VMEM((nz, heads * rows + 16, hd), BF16),
            pltpu.VMEM((NX, heads * rows + 8, hd), F32),
            pltpu.VMEM((nz, heads * rows, hd), BF16),
            pltpu.VMEM((nz, heads * rows, hd), BF16),
            pltpu.VMEM((nz, heads * rows, hd), F32),
            pltpu.VMEM((tokens, width), F32),
            pltpu.VMEM((ne, 32, width), BF16),
            pltpu.VMEM((ne, 32, width), BF16),
            dma((nz,)),
            dma((nz,)),
            dma((NX,)),
            dma((NX,)),
            dma((nz,)),
            dma((nz,)),
            dma((ne,)),
            dma((ne,)),
        ],
        compiler_params=pltpu.CompilerParams(
            collective_id=0, has_side_effects=True, vmem_limit_bytes=48 * 2**20
        ),
    )(q, k, v, ld, sin, routes, gain, gain4)


def experts_kernel(
    nz, unit_ref, gate_ref, up_ref, out_ref,
    bufa, bufb, wbuf, acc, own_sem, sa1, ra1, sa2, ra2, sb1, rb1, sb2, rb2,
):
    hidden = gate_ref.shape[1]
    depth = gate_ref.shape[2]
    quarter = depth // 4
    ka = bufa.shape[2]
    long, short = nz // 2, nz - 1 - nz // 2
    place = lax.axis_index("seq")
    x, z = place // nz, place % nz
    core = lax.axis_index("exp") % 2
    d = 1 - 2 * core

    def zat(k):
        return lax.rem(z + k * d + 2 * nz, nz)

    def xat(k):
        return lax.rem(x + k * d + 2 * NX, NX)

    loads = [
        pltpu.make_async_copy(unit_ref.at[:, pl.ds(0, ka)], bufa.at[z * NX + x], own_sem.at[0]),
        pltpu.make_async_copy(
            unit_ref.at[:, pl.ds(ka, unit_ref.shape[1] - ka)], bufb.at[z * NX + x], own_sem.at[1]
        ),
        pltpu.make_async_copy(gate_ref.at[0], wbuf.at[pl.ds(0, hidden)], own_sem.at[2]),
        pltpu.make_async_copy(up_ref.at[0], wbuf.at[pl.ds(hidden, hidden)], own_sem.at[3]),
    ]
    for c in loads:
        c.start()
    to_z = [{"seq": x * nz + zat(1)}, {"seq": x * nz + zat(-1)}]
    to_x = [{"seq": xat(j) * nz + z} for j in range(NX)]
    enter(to_z + to_x[1:])
    loads[0].wait()
    loads[1].wait()

    def a1(j):
        return remote(
            bufa.at[z * NX + x], bufa.at[z * NX + x], sa1.at[0], ra1.at[j - 1], to_x[j]
        )

    def a1_arrived(j):
        u = z * NX + xat(-j)
        return remote(bufa.at[u], bufa.at[u], sa1.at[0], ra1.at[j - 1], to_x[j])

    def a2(way, k, c):
        u = zat(-k if way == 0 else k) * NX + xat(-c)
        return remote(bufa.at[u], bufa.at[u], sa2.at[way], ra2.at[way, k, c], to_z[way])

    def a2_arrived(way, k, c):
        u = zat(-k - 1 if way == 0 else k + 1) * NX + xat(-c)
        return remote(bufa.at[u], bufa.at[u], sa2.at[way], ra2.at[way, k, c], to_z[way])

    def b1(way, k):
        u = zat(-k if way == 0 else k) * NX + x
        return remote(bufb.at[u], bufb.at[u], sb1.at[way], rb1.at[way, k], to_z[way])

    def b1_arrived(way, k):
        u = zat(-k - 1 if way == 0 else k + 1) * NX + x
        return remote(bufb.at[u], bufb.at[u], sb1.at[way], rb1.at[way, k], to_z[way])

    def b2(o, kind):
        u = zat(o) * NX + (x if kind < 2 else xat(-1))
        where = to_x[NX - 1] if kind == 1 else to_x[1]
        return remote(bufb.at[u], bufb.at[u], sb2.at[0], rb2.at[kind, o + nz], where)

    def b2_arrived(o, kind):
        u = zat(o) * NX + xat((-1, 1, -2)[kind])
        where = to_x[NX - 1] if kind == 1 else to_x[1]
        return remote(bufb.at[u], bufb.at[u], sb2.at[0], rb2.at[kind, o + nz], where)

    def spread(o):
        b2(o, 0).start()
        b2(o, 1).start()

    def forward(o):
        b2_arrived(o, 0).wait_recv()
        b2(o, 2).start()

    def finish(o):
        b2_arrived(o, 1).wait_recv()
        b2_arrived(o, 2).wait_recv()

    lanes = 16 * NX

    def compute(offsets):
        n = lanes * len(offsets)
        zs = [zat(o) for o in offsets]

        def stacked(buf, start, size):
            got = [
                buf[pl.ds(zz * NX, NX), :, start : start + size].reshape(lanes, size) for zz in zs
            ]
            return got[0] if len(got) == 1 else jnp.concatenate(got, axis=0)

        t = ((1,), (1,))
        main = dot(wbuf[:, 0:ka], stacked(bufa, 0, ka), t)
        main = main + dot(wbuf[:, ka:depth], stacked(bufb, 0, depth - ka), t)
        tail = stacked(bufb, depth - ka, quarter)
        lane = iota((2 * hidden, n), 1)
        rest = jnp.zeros((2 * hidden, n), F32)
        for g in range(4):
            one = dot(wbuf[:, g * quarter : (g + 1) * quarter], tail, t)
            rest = rest + jnp.where(lane % 16 // 4 == g, one, 0.0)
        if n < 128:
            rest = jnp.concatenate([rest, jnp.zeros((2 * hidden, 128 - n), F32)], axis=1)
            main = jnp.concatenate([main, jnp.zeros((2 * hidden, 128 - n), F32)], axis=1)
        rest = sum([pltpu.roll(rest, 4 * g, 1) for g in range(1, 4)], rest)

        def gated(a):
            gate, up = a[0:hidden], a[hidden : 2 * hidden]
            return (gate / (1.0 + jnp.exp(-gate)) * up).astype(BF16)

        columns = acc.shape[1]
        l = iota((128, columns), 0)
        r = l % 16
        start = zs[0] * CAP if len(zs) == 1 else jnp.where(l < lanes, zs[0], zs[1]) * CAP
        start = start + l % lanes // 16 * (nz * CAP)
        n_at = iota((128, columns), 1)
        used = l < n
        p_main = ((n_at == start + r) & used).astype(F32).astype(BF16)
        p_rest = ((n_at == start + 16 + r % 4) & (r >= 12) & used).astype(F32).astype(BF16)
        acc[...] += dot(gated(main), p_main) + dot(gated(rest), p_rest)

    acc[...] = jnp.zeros_like(acc)

    spread(0)
    for j in (1, 3, 2):
        a1(j).start()
    for way in range(2):
        b1(way, 0).start()
        a2(way, 0, 0).start()
    for c in (1, 3, 2):
        a1_arrived(c).wait_recv()
        for way in range(2):
            a2(way, 0, c).start()
    for way, o in ((0, -1), (1, 1)):
        b1_arrived(way, 0).wait_recv()
        b1(way, 1).start()
        spread(o)
    loads[2].wait()
    loads[3].wait()
    forward(0)

    def turn(t, first):
        for c in (0, 1):
            for way in range(2):
                a2_arrived(way, t - 1, c).wait_recv()
                a2(way, t, c).start()
        for way in range(2):
            b1_arrived(way, t).wait_recv()
            b1(way, t + 1).start()
            spread(-t - 1 if way == 0 else t + 1)
        for c in (3, 2):
            for way in range(2):
                a2_arrived(way, t - 1, c).wait_recv()
                a2(way, t, c).start()
        forward(-t)
        forward(t)
        if first:
            finish(0)
            compute([0])
        else:
            finish(1 - t)
            finish(t - 1)
            compute([1 - t, t - 1])

    turn(1, True)

    @pl.loop(2, short - 1)
    def _(t):
        turn(t, False)

    t = short - 1
    for c in (0, 1, 3, 2):
        for way in range(2):
            a2_arrived(way, t - 1, c).wait_recv()
            a2(way, t, c).start()
        if c == 1:
            b1_arrived(0, t).wait_recv()
            b1(0, t + 1).start()
            spread(-t - 1)
            b1_arrived(1, t).wait_recv()
            spread(t + 1)
    forward(-t)
    forward(t)
    finish(1 - t)
    finish(t - 1)
    compute([1 - t, t - 1])
    t = long - 1
    for c in (0, 1, 3, 2):
        a2_arrived(0, t - 1, c).wait_recv()
        a2(0, t, c).start()
        a2_arrived(1, t - 1, c).wait_recv()
        if c == 1:
            b1_arrived(0, t).wait_recv()
            spread(-t - 1)
    forward(-t)
    forward(t)
    finish(1 - t)
    finish(t - 1)
    compute([1 - t, t - 1])
    forward(-long)
    finish(-t)
    finish(t)
    compute([-t, t])
    for c in (0, 1, 3, 2):
        a2_arrived(0, t, c).wait_recv()
    finish(-long)
    compute([-long])
    out_ref[0] = acc[...].astype(BF16)

    def sent(buf, count, sem):
        span = buf.at[pl.ds(0, count)]
        remote(span, span, sem, ra1.at[0], to_z[0]).wait_send()

    sent(bufa, NX - 1, sa1.at[0])
    sent(bufa, NX * long, sa2.at[0])
    sent(bufa, NX * short, sa2.at[1])
    sent(bufb, long, sb1.at[0])
    sent(bufb, short, sb1.at[1])
    sent(bufb, 3 * nz, sb2.at[0])


def experts(nz, unit, w_gate, w_up):
    _, hidden, depth = w_gate.shape
    ka = depth * 22 // 48 // 128 * 128
    kb = unit.shape[1] - ka
    units = NX * nz
    long = nz // 2
    dma = pltpu.SemaphoreType.DMA
    anywhere = pl.BlockSpec(memory_space=pl.ANY)
    return pl.pallas_call(
        functools.partial(experts_kernel, nz),
        out_shape=jax.ShapeDtypeStruct((1, hidden, units * CAP), BF16),
        in_specs=[anywhere] * 3,
        out_specs=pl.BlockSpec(memory_space=pltpu.VMEM),
        scratch_shapes=[
            pltpu.VMEM((units, 16, ka), BF16),
            pltpu.VMEM((units, 16, kb), BF16),
            pltpu.VMEM((2 * hidden, depth), BF16),
            pltpu.VMEM((hidden, units * CAP), F32),
            dma((4,)),
            dma((1,)),
            dma((NX - 1,)),
            dma((2,)),
            dma((2, long, NX)),
            dma((2,)),
            dma((2, long)),
            dma((1,)),
            dma((3, 2 * nz)),
        ],
        compiler_params=pltpu.CompilerParams(
            collective_id=1, has_side_effects=True, vmem_limit_bytes=48 * 2**20
        ),
    )(unit, w_gate, w_up)


def shards(nz, ne, queries, keys, values, log_decay, state_in, norm_gain, routes, w_gate, w_up):
    heads, hd, _ = state_in.shape
    place = lax.axis_index("seq")
    rows = hd // nz
    part = rows // NX
    carried = lax.dynamic_slice_in_dim(
        state_in.reshape(heads, NX, hd // NX, hd), place % nz * part, part, 2
    ).reshape(heads * rows, hd)
    depth = norm_gain.shape[0]
    gain4 = jnp.repeat(norm_gain.reshape(4, depth // 4), 4, axis=0)
    unit, state_out = attend(
        nz, ne, queries, keys, values, log_decay, carried, routes.T, norm_gain[None], gain4
    )
    return experts(nz, unit, w_gate, w_up), state_out


def solution(mesh):
    placed = (
        P("seq", "exp"),
        P("seq", "exp"),
        P("seq", "exp"),
        P("exp", "seq"),
        P("exp", None, None),
        P(),
        P("seq", None),
        P("exp", "seq", None),
        P("exp", "seq", None),
    )
    return jax.shard_map(
        functools.partial(shards, mesh.shape["seq"] // NX, mesh.shape["exp"]),
        mesh=mesh,
        in_specs=placed,
        out_specs=(P("exp", "seq", None), P("exp", "seq", None)),
        check_vma=False,
    )
```

time: 849 us -> 167 us (0.20)
  waiting for transfers between devices: 634 us -> 0 us
  Pallas kernels: 0 us -> 154 us
  blocking collectives: 138 us -> 0 us
  matrix products: 22.5 us -> 0 us
  local copies, waits for them, and re-layouts: 28.1 us -> 10.9 us
  between operations: 15.2 us -> 0.71 us
    all_gather x2 -> x0, waiting for transfers between devices: 333 us -> none  [the longest x1 212 us: shards(): block_part = lax.all_gather(normed, 'seq', axis=1, tiled=True)]
    unnamed x4 -> x0, waiting for transfers between devices: 301 us -> none
    pallas_call x0 -> x2, Pallas kernels: none -> 154 us  [the longest x1 98 us: experts(): pl.pallas_call(functools.partial(experts_kernel, nz), out_shape=jax.Shape...]
    unnamed x1 -> x0, blocking collectives: 123 us -> none
    dot_general x6 -> x0, matrix products: 22.5 us -> none  [the longest x1 11 us: shards(): jnp.einsum('efd,end->efn', w_gate, block_part, preferred_element_type=jnp...]
    unnamed x10 -> x20, local copies, waits for them, and re-layouts: 25.5 us -> 10 us
    all_gather x1 -> x0, blocking collectives: 14.6 us -> none  [shards(): gathered = lax.all_gather(attended, 'exp', axis=1, tiled=True)]
  transfers between devices with their start and end apart: 3 -> 0, of which waited for: 3 -> 0; matrix products, arithmetic and copies ran while one was open for 1% -> 0% of each run, Pallas kernels for 0% -> 0%
where the time goes in v1:
time: 167 us; the launch traced here: 166 us
  Pallas kernels  154 us (92%)
  local copies, waits for them, and re-layouts  10.9 us (7%)
    pallas_call x1, Pallas kernels, experts(): pl.pallas_call(functools.partial(experts_kernel, nz), out_shape=jax.Shape...  98 us
    pallas_call x1, Pallas kernels, attend(): pl.pallas_call(functools.partial(attend_kernel, nz, ne), out_shape=(jax.S...  56.5 us
    unnamed x20, local copies, waits for them, and re-layouts  10 us

profile of v1, /device:TPU:1, one launch (start us, length us, event | category | flops | bytes accessed | tf_op | source)
XLA Modules:
  0.0 166.0 jit_solution(13377975885163808106)
XLA Ops:
  0.6 0.0 copy-start
  0.7 1.0 copy-done
  1.7 0.8 reshape.18
  2.5 0.0 copy-start.3
  2.5 0.9 copy-done.3
  3.4 0.0 copy-start.4
  3.4 0.9 copy-done.4
  4.3 0.0 copy-start.5
  4.3 0.9 copy-done.5
  5.2 0.0 copy-start.6
  5.2 0.7 copy-done.6
  5.9 0.0 copy-start.7
  5.9 0.7 copy-done.7
  6.6 0.0 copy-start.8
  6.6 0.7 copy-done.8
  7.3 56.5 %shard_map.104 = (bf16[16,7680]{1,0:T(8,128)(2,1)S(1)}, f32[6,2,128]{2,1,0:T(2,128)S(1)}) custom-call(bf16[64,768]{1,0:T(8,128)(2,1)S(1)} %copy-done.3, bf16[64,768]{1,0:T(8,128)(2,1)S(1)} %copy-done.4, bf16[64,768]{1,0:T(8,128)(2,1)S(1)} %copy-done.5, f32[6,64]{1,0:T(8,128)S(1)} %copy-done.7, f32[48,128]{1,0:T(8,128)S(1)} %bitcast.6, s32[2,64]{1,0:T(2,128)S(1)} %bitcast.7, ...), custom_call_target="tpu_custom_call" | custom-call | tf_op jit(solution)/shard_map/pallas_call | solution.py:238
  63.8 0.0 copy-start.1
  63.8 1.5 copy-done.1
  65.2 0.0 copy-start.2
  65.2 1.5 copy-done.2
  66.7 98.0 %shard_map.105 = bf16[1,144,1280]{2,1,0:T(8,128)(2,1)S(1)} custom-call(bf16[16,7680]{1,0:T(8,128)(2,1)S(1)} %get-tuple-element.4.unit_ref, bf16[1,144,6144]{2,1,0:T(8,128)(2,1)S(1)} %copy-done.1, bf16[1,144,6144]{2,1,0:T(8,128)(2,1)S(1)} %copy-done.2), custom_call_target="tpu_custom_call" | custom-call | tf_op jit(solution)/shard_map/pallas_call | solution.py:504
  164.7 0.7 copy.13
  165.5 0.6 copy.14
  (3 shorter events, 0.1 us)
Async XLA Ops:
  0.6 1.0 copy-start
  2.5 0.9 copy-start.3
  3.4 0.9 copy-start.4
  4.3 0.9 copy-start.5
  5.2 0.7 copy-start.6
  5.9 0.7 copy-start.7
  6.6 0.7 copy-start.8
  63.8 1.5 copy-start.1
  65.2 1.5 copy-start.2

commit v2 on v1

--- a/solution.py
+++ b/solution.py
@@ -37,12 +37,25 @@
     pl.semaphore_wait(barrier, len(peers))
 
 
-def attend_kernel(
-    nz, ne, q_ref, k_ref, v_ref, ld_ref, sin_ref, routes_ref, gain_ref, gain4_ref,
-    unit_ref, sout_ref,
-    stage, send1, recv1, xbuf, send2, recv2, ent, att, sende, recve,
-    s1, r1, sx_sem, rx_sem, s2, r2, se, re,
+def block_kernel(
+    nz, ne, q_hbm, k_hbm, v_hbm, ld_hbm, sin_hbm, routes_hbm, gain_hbm, gate_hbm, up_hbm,
+    out_ref, sout_ref,
+    q_ref, k_ref, v_ref, ld_ref, sin_ref, routes_ref, gain_ref, wbuf,
+    stage, send1, recv1, logs, xbuf, send2, recv2, ent, att, sende, recve,
+    bufa, bufb, acc,
+    load, sl, rl, s1, r1, sx_sem, rx_sem, s2, r2, se, re,
+    sa1, ra1, sa2, ra2, sb1, rb1, sb2, rb2,
 ):
+    hidden = gate_hbm.shape[1]
+    pairs = [
+        (q_hbm, q_ref), (k_hbm, k_ref), (v_hbm, v_ref), (ld_hbm, ld_ref), (sin_hbm, sin_ref),
+        (routes_hbm, routes_ref), (gain_hbm, gain_ref),
+        (gate_hbm.at[0], wbuf.at[pl.ds(0, hidden)]), (up_hbm.at[0], wbuf.at[pl.ds(hidden, hidden)]),
+    ]
+    loads = [pltpu.make_async_copy(a, b, load.at[i]) for i, (a, b) in enumerate(pairs)]
+    for c in loads:
+        c.start()
+
     tokens = q_ref.shape[0]
     heads = ld_ref.shape[0]
     hd = sin_ref.shape[1]
@@ -53,7 +66,8 @@
     place = lax.axis_index("seq")
     x, z = place // nz, place % nz
     me = lax.axis_index("exp")
-    zpeers = [(j, lax.rem(z + j, nz)) for j in range(1, nz)]
+    far = sorted(range(1, nz), key=lambda j: -min(j, nz - j))
+    zpeers = [(j, lax.rem(z + j, nz)) for j in far]
     xpeers = [(j, lax.rem(x + j, NX)) for j in range(1, NX)]
     epeers = [(j, lax.rem(me + j, ne)) for j in range(1, ne)]
     enter(
@@ -61,12 +75,24 @@
         + [{"seq": p * nz + z} for _, p in xpeers]
         + [{"exp": p} for _, p in epeers]
     )
+    for c in loads[:5]:
+        c.wait()
 
     ld = ld_ref[...]
     at_or_before = (iota((tokens, tokens), 0) <= iota((tokens, tokens), 1)).astype(F32)
     causal = iota((tokens, tokens), 0) >= iota((tokens, tokens), 1)
     cum = dot(ld, at_or_before, precision=HIGHEST)
     cumt = dot(causal.astype(F32), ld, ((1,), (1,)), HIGHEST)
+    lane = iota((1, hd), 1)
+    total = jnp.zeros((1, hd), F32)
+    for h in range(heads):
+        total = jnp.where(lane == h, cumt[tokens - 1 : tokens, h : h + 1], total)
+    logs[z] = total
+    pending = []
+    for j, p in zpeers:
+        c = remote(logs.at[z], logs.at[z], sl.at[j], rl.at[j], {"seq": x * nz + p})
+        c.start()
+        pending.append(c)
 
     d = iota((hd, hd), 0)
     per_x = hd // NX
@@ -78,7 +104,6 @@
 
     qs, ks = [], []
     for h in range(heads):
-        qs.append(dot(q_ref[:, cols(h)], perm).astype(BF16))
         ks.append(dot(k_ref[:, cols(h)], perm).astype(BF16))
     for h in range(heads):
         last = cum[h : h + 1, tokens - 1 : tokens]
@@ -88,27 +113,26 @@
         vh = v_ref[:, cols(h)]
         state = dot(high, vh, ((0,), (0,))) + dot(low, vh, ((0,), (0,)))
         stage[:, h * rows : (h + 1) * rows, :] = state.reshape(nz, rows, hd)
-    srows = heads * rows
-    send1[:, 0:srows, :] = stage[...].astype(BF16)
-    total = jnp.broadcast_to(cum[:, tokens - 1 : tokens], (heads, hd))
-    total = jnp.concatenate([total, jnp.zeros((8 - heads, hd), F32)], axis=0)
-    high = total.astype(BF16).astype(F32)
-    logs = jnp.concatenate([high, total - high], axis=0).astype(BF16)
-    send1[:, srows : srows + 16, :] = jnp.broadcast_to(logs[None], (nz, 16, hd))
-
-    firsts = []
+    send1[...] = stage[...].astype(BF16)
     for j, p in zpeers:
         c = remote(send1.at[p], recv1.at[z], s1.at[j], r1.at[j], {"seq": x * nz + p})
         c.start()
-        firsts.append(c)
+        pending.append(c)
     recv1[z] = send1[z]
 
     for h in range(heads):
+        qs.append(dot(q_ref[:, cols(h)], perm).astype(BF16))
         scores = dot(qs[h], ks[h], ((1,), (1,))) * scaling
         gap = cumt[:, h : h + 1] - cum[h : h + 1, :]
         weights = jnp.where(causal, jnp.exp(jnp.where(causal, gap, 0.0)), 0.0)
         att[:, cols(h)] = dot((scores * weights).astype(BF16), v_ref[:, cols(h)])
 
+    pick_r, pick_d = iota((rows, hd), 0), iota((rows, hd), 1)
+    pick = (pick_d == pick_r // part * per_x + z * part + pick_r % part).astype(F32)
+    first = [dot(pick, sin_ref[h], precision=HIGHEST) for h in range(heads)]
+
+    for c in loads[5:]:
+        c.wait()
     group = me // (ne // 4)
     expert = iota((ne, tokens), 0)
     chosen = (routes_ref[0:1, :] == expert) | (routes_ref[1:2, :] == expert)
@@ -124,57 +148,54 @@
         ],
         axis=0,
     )
-
+    acc[...] = jnp.zeros_like(acc)
+
+    for j, p in zpeers:
+        src = lax.rem(z + nz - j, nz)
+        remote(logs.at[src], logs.at[src], sl.at[j], rl.at[j], {"seq": x * nz + src}).wait_recv()
+    decays = [jnp.exp(logs[j]) for j in range(nz)]
+    whole = sum([logs[j] for j in range(nz)])
     for j, p in zpeers:
         src = lax.rem(z + nz - j, nz)
         remote(send1.at[src], recv1.at[src], s1.at[j], r1.at[j], {"seq": x * nz + src}).wait_recv()
 
-    def block(j):
-        piece = recv1[j].astype(F32)
-        logs = piece[srows : srows + 8] + piece[srows + 8 : srows + 16]
-        return piece, logs
-
     def step(running, piece, decay):
         return [
-            decay[h : h + 1, :] * running[h] + piece[h * rows : (h + 1) * rows]
+            decay[0:1, h : h + 1] * running[h] + piece[h * rows : (h + 1) * rows]
             for h in range(heads)
         ]
 
+    srows = heads * rows
     running = [jnp.zeros((rows, hd), F32)] * heads
-    whole = jnp.zeros((8, hd), F32)
     for j in range(nz):
-        piece, logs = block(j)
-        running = step(running, piece, jnp.exp(logs))
-        whole = whole + logs
+        running = step(running, recv1[j].astype(F32), decays[j])
     for h in range(heads):
         xbuf[x, h * rows : (h + 1) * rows, :] = running[h]
-    xbuf[x, srows : srows + 8, :] = whole
-    seconds = []
+    xbuf[x, srows : srows + 8, :] = jnp.broadcast_to(whole, (8, hd))
     for j, p in xpeers:
         c = remote(xbuf.at[x], xbuf.at[x], sx_sem.at[j], rx_sem.at[j], {"seq": p * nz + z})
         c.start()
-        seconds.append(c)
+        pending.append(c)
     for j, p in xpeers:
         src = lax.rem(x + NX - j, NX)
         remote(
             xbuf.at[src], xbuf.at[src], sx_sem.at[j], rx_sem.at[j], {"seq": src * nz + z}
         ).wait_recv()
 
-    final = [sin_ref[h * rows : (h + 1) * rows, :] for h in range(heads)]
-    entering = final
+    final = first
+    entering = first
     for g in range(NX):
         entering = [jnp.where(x == g, f, e) for f, e in zip(final, entering)]
         final = step(final, xbuf[g], jnp.exp(xbuf[g, srows : srows + 8, :]))
     for j in range(nz):
         send2[j] = jnp.concatenate(entering, axis=0).astype(BF16)
+
+        @pl.when(z != j)
+        def _(j=j):
+            remote(send2.at[j], recv2.at[z], s2.at[j], r2.at[z], {"seq": x * nz + j}).start()
+
         if j < nz - 1:
-            piece, logs = block(j)
-            entering = step(entering, piece, jnp.exp(logs))
-    thirds = []
-    for j, p in zpeers:
-        c = remote(send2.at[p], recv2.at[z], s2.at[j], r2.at[j], {"seq": x * nz + p})
-        c.start()
-        thirds.append(c)
+            entering = step(entering, recv1[j].astype(F32), decays[j])
     recv2[z] = send2[z]
     for h in range(heads):
         mine = jnp.zeros((part, hd), F32)
@@ -182,8 +203,7 @@
             mine = jnp.where(x == g, final[h][g * part : (g + 1) * part], mine)
         sout_ref[h] = mine
     for j, p in zpeers:
-        src = lax.rem(z + nz - j, nz)
-        remote(send2.at[src], recv2.at[src], s2.at[j], r2.at[j], {"seq": x * nz + src}).wait_recv()
+        remote(send2.at[p], recv2.at[p], s2.at[p], r2.at[p], {"seq": x * nz + p}).wait_recv()
 
     ent[...] = recv2[...].astype(F32)
     parts = []
@@ -194,94 +214,50 @@
     attended = jnp.concatenate(parts, axis=1)
     for e in range(ne):
         sende[e] = dot(selector[e * 32 : (e + 1) * 32], attended).astype(BF16)
-    fourths = []
     for j, p in epeers:
         c = remote(sende.at[p], recve.at[me], se.at[j], re.at[j], {"exp": p})
         c.start()
-        fourths.append(c)
+        pending.append(c)
     recve[me] = sende[me]
     for j, p in epeers:
         src = lax.rem(me + ne - j, ne)
         remote(sende.at[src], recve.at[src], se.at[j], re.at[j], {"exp": src}).wait_recv()
 
     depth = ne * width
+    quarter = depth // 4
+    ka = bufa.shape[2]
+    own = z * NX + x
+
+    def put(start, value):
+        cut = min(max(ka - start, 0), value.shape[1])
+        if cut > 0:
+            bufa[own, :, start : start + cut] = value[:, 0:cut]
+        if cut < value.shape[1]:
+            bufb[own, :, start + cut - ka : start + value.shape[1] - ka] = value[:, cut:]
+
     wide = [recve[e].astype(F32) for e in range(ne)]
     main = [w[0:16] for w in wide]
     halves = ne // 4
-    rest = [sum(wide[g * halves + i][16:32] for g in range(4)) for i in range(halves)]
-    square = sum(jnp.sum(m * m, axis=1, keepdims=True) for m in main)
+    rest = [sum([wide[g * halves + i][16:32] for g in range(4)]) for i in range(halves)]
+    square = sum([jnp.sum(m * m, axis=1, keepdims=True) for m in main])
     scale = lax.rsqrt(square / depth + EPSILON)
     for e in range(ne):
         at = slice(e * width, (e + 1) * width)
-        unit_ref[:, at] = (main[e] * scale * gain_ref[:, at]).astype(BF16)
-    square = sum(jnp.sum(m * m, axis=1, keepdims=True) for m in rest)
+        put(e * width, (main[e] * scale * gain_ref[:, at]).astype(BF16))
+    square = sum([jnp.sum(m * m, axis=1, keepdims=True) for m in rest])
     same = (iota((16, 16), 0) % 4 == iota((16, 16), 1) % 4).astype(F32)
     square = dot(same, jnp.broadcast_to(square, (16, 128)), precision=HIGHEST)[:, 0:1]
     scale = lax.rsqrt(square / depth + EPSILON)
+    line = iota((16, width), 0) // 4
     for i in range(halves):
-        at = slice(i * width, (i + 1) * width)
-        unit_ref[:, depth + i * width : depth + (i + 1) * width] = (
-            rest[i] * scale * gain4_ref[:, at]
-        ).astype(BF16)
-
-    for c in firsts + seconds + thirds + fourths:
-        c.wait_send()
-
-
-def attend(nz, ne, q, k, v, ld, sin, routes, gain, gain4):
-    tokens, width = q.shape
-    heads, hd = ld.shape[0], sin.shape[1]
-    rows = hd // nz
-    depth = ne * width
-    dma = pltpu.SemaphoreType.DMA
-    vmem = pl.BlockSpec(memory_space=pltpu.VMEM)
-    return pl.pallas_call(
-        functools.partial(attend_kernel, nz, ne),
-        out_shape=(
-            jax.ShapeDtypeStruct((16, depth + depth // 4), BF16),
-            jax.ShapeDtypeStruct((heads, rows // NX, hd), F32),
-        ),
-        in_specs=[vmem] * 8,
-        out_specs=(vmem, vmem),
-        scratch_shapes=[
-            pltpu.VMEM((nz, heads * rows, hd), F32),
-            pltpu.VMEM((nz, heads * rows + 16, hd), BF16),
-            pltpu.VMEM((nz, heads * rows + 16, hd), BF16),
-            pltpu.VMEM((NX, heads * rows + 8, hd), F32),
-            pltpu.VMEM((nz, heads * rows, hd), BF16),
-            pltpu.VMEM((nz, heads * rows, hd), BF16),
-            pltpu.VMEM((nz, heads * rows, hd), F32),
-            pltpu.VMEM((tokens, width), F32),
-            pltpu.VMEM((ne, 32, width), BF16),
-            pltpu.VMEM((ne, 32, width), BF16),
-            dma((nz,)),
-            dma((nz,)),
-            dma((NX,)),
-            dma((NX,)),
-            dma((nz,)),
-            dma((nz,)),
-            dma((ne,)),
-            dma((ne,)),
-        ],
-        compiler_params=pltpu.CompilerParams(
-            collective_id=0, has_side_effects=True, vmem_limit_bytes=48 * 2**20
-        ),
-    )(q, k, v, ld, sin, routes, gain, gain4)
-
-
-def experts_kernel(
-    nz, unit_ref, gate_ref, up_ref, out_ref,
-    bufa, bufb, wbuf, acc, own_sem, sa1, ra1, sa2, ra2, sb1, rb1, sb2, rb2,
-):
-    hidden = gate_ref.shape[1]
-    depth = gate_ref.shape[2]
-    quarter = depth // 4
-    ka = bufa.shape[2]
+        gain = jnp.zeros((16, width), F32)
+        for g in range(4):
+            at = g * quarter + i * width
+            gain = jnp.where(line == g, gain_ref[:, at : at + width], gain)
+        put(depth + i * width, (rest[i] * scale * gain).astype(BF16))
+
     long, short = nz // 2, nz - 1 - nz // 2
-    place = lax.axis_index("seq")
-    x, z = place // nz, place % nz
-    core = lax.axis_index("exp") % 2
-    d = 1 - 2 * core
+    d = 1 - 2 * (me % 2)
 
     def zat(k):
         return lax.rem(z + k * d + 2 * nz, nz)
@@ -289,21 +265,8 @@
     def xat(k):
         return lax.rem(x + k * d + 2 * NX, NX)
 
-    loads = [
-        pltpu.make_async_copy(unit_ref.at[:, pl.ds(0, ka)], bufa.at[z * NX + x], own_sem.at[0]),
-        pltpu.make_async_copy(
-            unit_ref.at[:, pl.ds(ka, unit_ref.shape[1] - ka)], bufb.at[z * NX + x], own_sem.at[1]
-        ),
-        pltpu.make_async_copy(gate_ref.at[0], wbuf.at[pl.ds(0, hidden)], own_sem.at[2]),
-        pltpu.make_async_copy(up_ref.at[0], wbuf.at[pl.ds(hidden, hidden)], own_sem.at[3]),
-    ]
-    for c in loads:
-        c.start()
     to_z = [{"seq": x * nz + zat(1)}, {"seq": x * nz + zat(-1)}]
     to_x = [{"seq": xat(j) * nz + z} for j in range(NX)]
-    enter(to_z + to_x[1:])
-    loads[0].wait()
-    loads[1].wait()
 
     def a1(j):
         return remote(
@@ -392,8 +355,6 @@
         p_main = ((n_at == start + r) & used).astype(F32).astype(BF16)
         p_rest = ((n_at == start + 16 + r % 4) & (r >= 12) & used).astype(F32).astype(BF16)
         acc[...] += dot(gated(main), p_main) + dot(gated(rest), p_rest)
-
-    acc[...] = jnp.zeros_like(acc)
 
     spread(0)
     for j in (1, 3, 2):
@@ -409,8 +370,6 @@
         b1_arrived(way, 0).wait_recv()
         b1(way, 1).start()
         spread(o)
-    loads[2].wait()
-    loads[3].wait()
     forward(0)
 
     def turn(t, first):
@@ -491,56 +450,83 @@
     sent(bufb, long, sb1.at[0])
     sent(bufb, short, sb1.at[1])
     sent(bufb, 3 * nz, sb2.at[0])
-
-
-def experts(nz, unit, w_gate, w_up):
+    for c in pending:
+        c.wait_send()
+    for j, p in zpeers:
+        remote(send2.at[p], recv2.at[p], s2.at[p], r2.at[p], {"seq": x * nz + p}).wait_send()
+
+
+def block(nz, ne, q, k, v, ld, sin, routes, gain, w_gate, w_up):
+    tokens, width = q.shape
+    heads, hd = ld.shape[0], sin.shape[1]
+    rows = hd // nz
     _, hidden, depth = w_gate.shape
+    units = NX * nz
     ka = depth * 22 // 48 // 128 * 128
-    kb = unit.shape[1] - ka
-    units = NX * nz
-    long = nz // 2
+    kb = depth + depth // 4 - ka
     dma = pltpu.SemaphoreType.DMA
-    anywhere = pl.BlockSpec(memory_space=pl.ANY)
+    vmem = pl.BlockSpec(memory_space=pltpu.VMEM)
     return pl.pallas_call(
-        functools.partial(experts_kernel, nz),
-        out_shape=jax.ShapeDtypeStruct((1, hidden, units * CAP), BF16),
-        in_specs=[anywhere] * 3,
-        out_specs=pl.BlockSpec(memory_space=pltpu.VMEM),
+        functools.partial(block_kernel, nz, ne),
+        out_shape=(
+            jax.ShapeDtypeStruct((1, hidden, units * CAP), BF16),
+            jax.ShapeDtypeStruct((heads, rows // NX, hd), F32),
+        ),
+        in_specs=[pl.BlockSpec(memory_space=pl.ANY)] * 9,
+        out_specs=(vmem, vmem),
         scratch_shapes=[
+            pltpu.VMEM(q.shape, BF16),
+            pltpu.VMEM(k.shape, BF16),
+            pltpu.VMEM(v.shape, BF16),
+            pltpu.VMEM(ld.shape, F32),
+            pltpu.VMEM(sin.shape, F32),
+            pltpu.VMEM(routes.shape, jnp.int32),
+            pltpu.VMEM(gain.shape, F32),
+            pltpu.VMEM((2 * hidden, depth), BF16),
+            pltpu.VMEM((nz, heads * rows, hd), F32),
+            pltpu.VMEM((nz, heads * rows, hd), BF16),
+            pltpu.VMEM((nz, heads * rows, hd), BF16),
+            pltpu.VMEM((nz, 1, hd), F32),
+            pltpu.VMEM((NX, heads * rows + 8, hd), F32),
+            pltpu.VMEM((nz, heads * rows, hd), BF16),
+            pltpu.VMEM((nz, heads * rows, hd), BF16),
+            pltpu.VMEM((nz, heads * rows, hd), F32),
+            pltpu.VMEM((tokens, width), F32),
+            pltpu.VMEM((ne, 32, width), BF16),
+            pltpu.VMEM((ne, 32, width), BF16),
             pltpu.VMEM((units, 16, ka), BF16),
             pltpu.VMEM((units, 16, kb), BF16),
-            pltpu.VMEM((2 * hidden, depth), BF16),
             pltpu.VMEM((hidden, units * CAP), F32),
-            dma((4,)),
+            dma((9,)),
+            dma((nz,)),
+            dma((nz,)),
+            dma((nz,)),
+            dma((nz,)),
+            dma((NX,)),
+            dma((NX,)),
+            dma((nz,)),
+            dma((nz,)),
+            dma((ne,)),
+            dma((ne,)),
             dma((1,)),
             dma((NX - 1,)),
             dma((2,)),
-            dma((2, long, NX)),
+            dma((2, nz // 2, NX)),
             dma((2,)),
-            dma((2, long)),
+            dma((2, nz // 2)),
             dma((1,)),
             dma((3, 2 * nz)),
         ],
         compiler_params=pltpu.CompilerParams(
-            collective_id=1, has_side_effects=True, vmem_limit_bytes=48 * 2**20
+            collective_id=0, has_side_effects=True, vmem_limit_bytes=60 * 2**20
         ),
-    )(unit, w_gate, w_up)
+    )(q, k, v, ld, sin, routes, gain, w_gate, w_up)
 
 
 def shards(nz, ne, queries, keys, values, log_decay, state_in, norm_gain, routes, w_gate, w_up):
-    heads, hd, _ = state_in.shape
-    place = lax.axis_index("seq")
-    rows = hd // nz
-    part = rows // NX
-    carried = lax.dynamic_slice_in_dim(
-        state_in.reshape(heads, NX, hd // NX, hd), place % nz * part, part, 2
-    ).reshape(heads * rows, hd)
-    depth = norm_gain.shape[0]
-    gain4 = jnp.repeat(norm_gain.reshape(4, depth // 4), 4, axis=0)
-    unit, state_out = attend(
-        nz, ne, queries, keys, values, log_decay, carried, routes.T, norm_gain[None], gain4
+    return block(
+        nz, ne, queries, keys, values, log_decay, state_in, routes.T, norm_gain[None], w_gate, w_up
     )
-    return experts(nz, unit, w_gate, w_up), state_out
 
 
 def solution(mesh):

time: 167 us -> 152 us (0.910)
  local copies, waits for them, and re-layouts: 10.9 us -> 3.03 us
  Pallas kernels: 154 us -> 147 us
    pallas_call x2 -> x1, Pallas kernels: 154 us -> 147 us  [block(): pl.pallas_call(functools.partial(block_kernel, nz, ne), out_shape=(jax.Sh...]
    unnamed x20 -> x2, local copies, waits for them, and re-layouts: 10 us -> 3.03 us
where the time goes in v2:
time: 152 us; the launch traced here: 151 us
  Pallas kernels  147 us (97%)
  local copies, waits for them, and re-layouts  3.03 us (2%)
    pallas_call x1, Pallas kernels, block(): pl.pallas_call(functools.partial(block_kernel, nz, ne), out_shape=(jax.Sh...  147 us

profile of v2, /device:TPU:1, one launch (start us, length us, event | category | flops | bytes accessed | tf_op | source)
XLA Modules:
  0.0 151.1 jit_solution(2077817668437736041)
XLA Ops:
  0.6 147.4 %shard_map.104 = (bf16[1,144,1280]{2,1,0:T(8,128)(2,1)}, f32[6,2,128]{2,1,0:T(2,128)}) custom-call(bf16[64,768]{1,0:T(8,128)(2,1)} %q_hbm.1, bf16[64,768]{1,0:T(8,128)(2,1)} %k_hbm.1, bf16[64,768]{1,0:T(8,128)(2,1)} %v_hbm.1, f32[6,64]{1,0:T(8,128)} %ld_hbm.1, f32[6,128,128]{2,1,0:T(8,128)} %sin_hbm.1, s32[2,64]{1,0:T(2,128)} %bitcast.3, f32[1,6144]{1,0:T(1,128)} %bitcast.2, ...), custom_call_target="tpu_custom_call" | custom-call | tf_op jit(solution)/shard_map/pallas_call | solution.py:469
  148.1 1.7 %copy.13 = bf16[1,144,1280]{2,1,0:T(8,128)(2,1)} copy(bf16[1,144,1280]{2,1,0:T(8,128)(2,1)} %get-tuple-element.4) | data formatting | bytes 737280
  149.8 1.3 copy.14

commit v3 on v2

--- a/solution.py
+++ b/solution.py
@@ -41,10 +41,10 @@
     nz, ne, q_hbm, k_hbm, v_hbm, ld_hbm, sin_hbm, routes_hbm, gain_hbm, gate_hbm, up_hbm,
     out_ref, sout_ref,
     q_ref, k_ref, v_ref, ld_ref, sin_ref, routes_ref, gain_ref, wbuf,
-    stage, send1, recv1, logs, xbuf, send2, recv2, ent, att, sende, recve,
-    bufa, bufb, acc,
-    load, sl, rl, s1, r1, sx_sem, rx_sem, s2, r2, se, re,
-    sa1, ra1, sa2, ra2, sb1, rb1, sb2, rb2,
+    stage, send1, recv1, logs, xbuf, send2, recv2, ent, att, sende, recve, squares, whole_att, raw,
+    bufa, bufb, tokb, acc,
+    load, sl, rl, s1, r1, sx_sem, rx_sem, s2, r2, se, re, sq, rq, sr, rr,
+    sa1, ra1, st1, rt1, sa2, ra2, st2, rt2, sb1, rb1, sb2, rb2, sy, ry, ss, rs,
 ):
     hidden = gate_hbm.shape[1]
     pairs = [
@@ -133,21 +133,18 @@
 
     for c in loads[5:]:
         c.wait()
-    group = me // (ne // 4)
     expert = iota((ne, tokens), 0)
     chosen = (routes_ref[0:1, :] == expert) | (routes_ref[1:2, :] == expert)
     position = dot(chosen.astype(F32), at_or_before, precision=HIGHEST) - 1.0
     position = jnp.where(chosen, position, -1.0)
-    line = iota((32, tokens), 0)
-    slot = jnp.where(line < 16, line, jnp.where((line - 16) // 4 == group, 16 + line % 4, -5))
+    line = iota((48, tokens), 0)
+    group = (2 * me + line // 32) // 3
+    slot = jnp.where(line < 16, line, jnp.where(line % 16 // 4 == group, 16 + line % 4, -5))
     slot = slot.astype(F32)
-    selector = jnp.concatenate(
-        [
-            (jnp.abs(slot - position[e : e + 1, :]) < 0.5).astype(F32).astype(BF16)
-            for e in range(ne)
-        ],
-        axis=0,
-    )
+    selectors = [
+        (jnp.abs(slot - position[e : e + 1, :]) < 0.5).astype(F32).astype(BF16) for e in range(ne)
+    ]
+    slots = jnp.sum(jnp.where(expert == me, position, 0.0), axis=0, keepdims=True)
     acc[...] = jnp.zeros_like(acc)
 
     for j, p in zpeers:
@@ -212,52 +209,107 @@
         carried = dot(qs[h], state) * scaling * jnp.exp(cumt[:, h : h + 1])
         parts.append((att[:, cols(h)] + carried).astype(BF16))
     attended = jnp.concatenate(parts, axis=1)
-    for e in range(ne):
-        sende[e] = dot(selector[e * 32 : (e + 1) * 32], attended).astype(BF16)
+    y, core = me // 2, me % 2
+    by_rows = ne - 2
+    wide = attended.astype(F32)
+    square = dot(jnp.ones((8, width), F32), wide * wide, ((1,), (1,)), HIGHEST)[0:1]
+    squares[me] = jnp.concatenate([square, jnp.zeros((1, hd - tokens), F32)], axis=1)
     for j, p in epeers:
-        c = remote(sende.at[p], recve.at[me], se.at[j], re.at[j], {"exp": p})
+        c = remote(squares.at[me], squares.at[me], sq.at[j], rq.at[j], {"exp": p})
         c.start()
         pending.append(c)
-    recve[me] = sende[me]
+    ny = ne // 2
+    whole_att[...] = attended.reshape(ny, tokens // ny, width)
+
+    def raw_to(t):
+        return remote(whole_att.at[t], raw.at[0], sr.at[t], rr.at[0], {"exp": 2 * t + core})
+
+    @pl.when(me >= by_rows)
+    def _():
+        for t in range(ny - 1):
+            raw_to(t).start()
+        raw[0] = whole_att[ny - 1]
+
+    half = width // 2
+    for e in range(ne):
+        picked = dot(selectors[e], attended).astype(BF16)
+        last = jnp.concatenate([picked[16:32, 0:half], picked[32:48, half:width]], axis=1)
+        sende[e] = jnp.concatenate([picked[0:16], last], axis=0)
+
+    def rows_to(j, p):
+        return remote(sende.at[p], recve.at[me], se.at[j], re.at[me], {"exp": p})
+
+    @pl.when(me < by_rows)
+    def _():
+        for j, p in epeers:
+            rows_to(j, p).start()
+        recve[me] = sende[me]
+
     for j, p in epeers:
         src = lax.rem(me + ne - j, ne)
-        remote(sende.at[src], recve.at[src], se.at[j], re.at[j], {"exp": src}).wait_recv()
+        remote(squares.at[src], squares.at[src], sq.at[j], rq.at[j], {"exp": src}).wait_recv()
 
     depth = ne * width
-    quarter = depth // 4
-    ka = bufa.shape[2]
+    deep = by_rows * width
+    quarter = deep // 4
+    ka = bufa.shape[2] - 128
     own = z * NX + x
+    square = sum([squares[e] for e in range(ne)])[:, 0:tokens]
+    scale = lax.rsqrt(square / depth + EPSILON)
+    line = iota((32, tokens), 0)
+    slot = jnp.where(line < 16, line, 16 + line % 4).astype(F32)
+    hit = jnp.abs(slot - slots) < 0.5
+    row_scale = jnp.sum(jnp.where(hit, scale, 0.0), axis=1, keepdims=True)
+    line = iota((16, tokens), 0)
+    hit = iota((16, tokens), 1) == y * 16 + line
+    tok_scale = jnp.sum(jnp.where(hit, scale, 0.0), axis=1, keepdims=True)
+
+    lane = iota((tokens, NX * tokens), 1)
+    spot = (lane // 16 % NX == x) & (lane // (16 * NX) * 16 + lane % 16 == iota(lane.shape, 0))
+    named = jnp.broadcast_to((slots + 1.0).astype(BF16), (16, tokens))
+    named = dot(named, spot.astype(F32).astype(BF16))
+    line = iota((16, 128), 0)
+    named = jnp.where(line == 0, named[:, 0:128], jnp.where(line == 1, named[:, 128:256], 0.0))
+    bufa[own, :, ka : ka + 128] = named.astype(BF16)
+
+    @pl.when(me < by_rows)
+    def _():
+        remote(raw.at[0], raw.at[0], sr.at[0], rr.at[0], {"exp": by_rows + core}).wait_recv()
+
+    at = depth - 2 * width
+    gain = jnp.where(
+        core == 0, gain_ref[:, at : at + width], gain_ref[:, at + width : at + 2 * width]
+    )
+    tokb[core * ny + y, own] = (raw[0].astype(F32) * tok_scale * gain).astype(BF16)
+
+    for src in range(by_rows):
+
+        @pl.when(me != src)
+        def _(src=src):
+            remote(recve.at[src], recve.at[src], se.at[0], re.at[src], {"exp": src}).wait_recv()
 
     def put(start, value):
-        cut = min(max(ka - start, 0), value.shape[1])
-        if cut > 0:
-            bufa[own, :, start : start + cut] = value[:, 0:cut]
-        if cut < value.shape[1]:
-            bufb[own, :, start + cut - ka : start + value.shape[1] - ka] = value[:, cut:]
-
-    wide = [recve[e].astype(F32) for e in range(ne)]
-    main = [w[0:16] for w in wide]
-    halves = ne // 4
-    rest = [sum([wide[g * halves + i][16:32] for g in range(4)]) for i in range(halves)]
-    square = sum([jnp.sum(m * m, axis=1, keepdims=True) for m in main])
-    scale = lax.rsqrt(square / depth + EPSILON)
-    for e in range(ne):
-        at = slice(e * width, (e + 1) * width)
-        put(e * width, (main[e] * scale * gain_ref[:, at]).astype(BF16))
-    square = sum([jnp.sum(m * m, axis=1, keepdims=True) for m in rest])
-    same = (iota((16, 16), 0) % 4 == iota((16, 16), 1) % 4).astype(F32)
-    square = dot(same, jnp.broadcast_to(square, (16, 128)), precision=HIGHEST)[:, 0:1]
-    scale = lax.rsqrt(square / depth + EPSILON)
-    line = iota((16, width), 0) // 4
-    for i in range(halves):
-        gain = jnp.zeros((16, width), F32)
+        if start < ka:
+            bufa[own, :, start : start + value.shape[1]] = value
+        else:
+            bufb[own, :, start - ka : start - ka + value.shape[1]] = value
+
+    for e in range(by_rows):
+        gain = gain_ref[:, e * width : (e + 1) * width]
+        put(e * width, (recve[e, 0:16].astype(F32) * row_scale[0:16] * gain).astype(BF16))
+    line = iota((16, half), 0) // 4
+    for i in range(3):
+        gain = jnp.zeros((16, half), F32)
+        rest = jnp.zeros((16, half), F32)
         for g in range(4):
-            at = g * quarter + i * width
-            gain = jnp.where(line == g, gain_ref[:, at : at + width], gain)
-        put(depth + i * width, (rest[i] * scale * gain).astype(BF16))
+            at = g * quarter + i * half
+            gain = jnp.where(line == g, gain_ref[:, at : at + half], gain)
+            e, side = (3 * g + i) // 2, (3 * g + i) % 2 * half
+            rest = rest + recve[e, 16:32, side : side + half].astype(F32)
+        put(deep + i * half, (rest * row_scale[16:32] * gain).astype(BF16))
 
     long, short = nz // 2, nz - 1 - nz // 2
-    d = 1 - 2 * (me % 2)
+    d = 1 - 2 * core
 
     def zat(k):
         return lax.rem(z + k * d + 2 * nz, nz)
@@ -268,22 +320,49 @@
     to_z = [{"seq": x * nz + zat(1)}, {"seq": x * nz + zat(-1)}]
     to_x = [{"seq": xat(j) * nz + z} for j in range(NX)]
 
-    def a1(j):
-        return remote(
-            bufa.at[z * NX + x], bufa.at[z * NX + x], sa1.at[0], ra1.at[j - 1], to_x[j]
-        )
-
-    def a1_arrived(j):
-        u = z * NX + xat(-j)
+    to_y = [{"exp": lax.rem(y + j * d + ny, ny) * 2 + core} for j in (1, -1)]
+    sibling = {"exp": me + d}
+
+    def columns(o):
+        return pl.ds(zat(o) * NX, NX)
+
+    def a1(j, back):
+        u = z * NX + xat(-back)
         return remote(bufa.at[u], bufa.at[u], sa1.at[0], ra1.at[j - 1], to_x[j])
 
-    def a2(way, k, c):
-        u = zat(-k if way == 0 else k) * NX + xat(-c)
+    def t1(j, back):
+        part = tokb.at[core * ny + y, z * NX + xat(-back)]
+        return remote(part, part, st1.at[0], rt1.at[j - 1], to_x[j])
+
+    def a2(way, k, c, ahead=0):
+        u = zat(-k - ahead if way == 0 else k + ahead) * NX + xat(-c)
         return remote(bufa.at[u], bufa.at[u], sa2.at[way], ra2.at[way, k, c], to_z[way])
 
-    def a2_arrived(way, k, c):
-        u = zat(-k - 1 if way == 0 else k + 1) * NX + xat(-c)
-        return remote(bufa.at[u], bufa.at[u], sa2.at[way], ra2.at[way, k, c], to_z[way])
+    def t2(way, k, c, ahead=0):
+        u = zat(-k - ahead if way == 0 else k + ahead) * NX + xat(-c)
+        part = tokb.at[core * ny + y, u]
+        return remote(part, part, st2.at[way], rt2.at[way, k, c], to_z[way])
+
+    def tok_y(o, kind, back):
+        part = tokb.at[core * ny + lax.rem(y - back * d + 2 * ny, ny), columns(o)]
+        return remote(part, part, sy.at[0], ry.at[kind, o + nz], to_y[1 if kind == 1 else 0])
+
+    def tok_core(o, whose):
+        part = tokb.at[pl.ds(whose * ny, ny), columns(o)]
+        return remote(part, part, ss.at[0], rs.at[o + nz], sibling)
+
+    def y_spread(o):
+        tok_y(o, 0, 0).start()
+        tok_y(o, 1, 0).start()
+
+    def y_forward(o):
+        tok_y(o, 0, 1).wait_recv()
+        tok_y(o, 2, 1).start()
+
+    def y_share(o):
+        tok_y(o, 1, -1).wait_recv()
+        tok_y(o, 2, 2).wait_recv()
+        tok_core(o, core).start()
 
     def b1(way, k):
         u = zat(-k if way == 0 else k) * NX + x
@@ -314,6 +393,7 @@
     def finish(o):
         b2_arrived(o, 1).wait_recv()
         b2_arrived(o, 2).wait_recv()
+        tok_core(o, 1 - core).wait_recv()
 
     lanes = 16 * NX
 
@@ -329,13 +409,36 @@
 
         t = ((1,), (1,))
         main = dot(wbuf[:, 0:ka], stacked(bufa, 0, ka), t)
-        main = main + dot(wbuf[:, ka:depth], stacked(bufb, 0, depth - ka), t)
-        tail = stacked(bufb, depth - ka, quarter)
+        main = main + dot(wbuf[:, ka:deep], stacked(bufb, 0, deep - ka), t)
+        tail = stacked(bufb, deep - ka, quarter)
         lane = iota((2 * hidden, n), 1)
         rest = jnp.zeros((2 * hidden, n), F32)
         for g in range(4):
             one = dot(wbuf[:, g * quarter : (g + 1) * quarter], tail, t)
             rest = rest + jnp.where(lane % 16 // 4 == g, one, 0.0)
+        span = NX * tokens
+        line, key = iota((2 * lanes, span), 0), iota((2 * lanes, span), 1)
+        r = line % 16
+        want = jnp.where(line < lanes, r + 1, jnp.where(r >= 12, r + 5, -5))
+        want = jnp.where(line % lanes // 16 == key // 16 % NX, want, -5).astype(F32)
+        picked = [[], []]
+        for zz in zs:
+            tile = bufa[pl.ds(zz * NX, NX), :, ka : ka + 128].astype(F32).sum(axis=0)
+            named = jnp.concatenate([tile[0:1], tile[1:2]], axis=1)
+            pick = (jnp.abs(want - named) < 0.5).astype(F32).astype(BF16)
+            for i in range(2):
+                source = jnp.concatenate(
+                    [
+                        tokb[i * ny + t, pl.ds(zz * NX, NX)].reshape(NX * 16, width)
+                        for t in range(ny)
+                    ],
+                    axis=0,
+                )
+                picked[i].append(dot(pick, source).astype(BF16))
+        for i in range(2):
+            w = wbuf[:, deep + i * width : deep + (i + 1) * width]
+            main = main + dot(w, jnp.concatenate([p[0:lanes] for p in picked[i]], axis=0), t)
+            rest = rest + dot(w, jnp.concatenate([p[lanes:] for p in picked[i]], axis=0), t)
         if n < 128:
             rest = jnp.concatenate([rest, jnp.zeros((2 * hidden, 128 - n), F32)], axis=1)
             main = jnp.concatenate([main, jnp.zeros((2 * hidden, 128 - n), F32)], axis=1)
@@ -358,84 +461,85 @@
 
     spread(0)
     for j in (1, 3, 2):
-        a1(j).start()
+        t1(j, 0).start()
     for way in range(2):
         b1(way, 0).start()
+        t2(way, 0, 0).start()
         a2(way, 0, 0).start()
-    for c in (1, 3, 2):
-        a1_arrived(c).wait_recv()
+    for j in (1, 3, 2):
+        a1(j, 0).start()
+    for j in (1, 3, 2):
+        t1(j, j).wait_recv()
         for way in range(2):
-            a2(way, 0, c).start()
+            t2(way, 0, j).start()
+    y_spread(0)
+    for j in (1, 3, 2):
+        a1(j, j).wait_recv()
+        for way in range(2):
+            a2(way, 0, j).start()
     for way, o in ((0, -1), (1, 1)):
         b1_arrived(way, 0).wait_recv()
         b1(way, 1).start()
         spread(o)
+    for c in (0, 1, 3, 2):
+        for way in range(2):
+            t2(way, 0, c, 1).wait_recv()
+            t2(way, 1, c).start()
+    y_spread(-1)
+    y_spread(1)
     forward(0)
-
-    def turn(t, first):
-        for c in (0, 1):
+    y_forward(0)
+
+    def turn(t, first=False, both=True, ahead=(True, True)):
+        ways = (0, 1) if both else (0,)
+        for c in (0, 1, 3, 2):
+            for way in ways:
+                t2(way, t, c, 1).wait_recv()
+                if ahead[way]:
+                    t2(way, t + 1, c).start()
+        for way in ways:
+            y_spread(-t - 1 if way == 0 else t + 1)
+        for way in ways:
+            o = -t - 1 if way == 0 else t + 1
+            b1_arrived(way, t).wait_recv()
+            if ahead[way]:
+                b1(way, t + 1).start()
+            spread(o)
+        for c in (0, 1, 3, 2):
             for way in range(2):
-                a2_arrived(way, t - 1, c).wait_recv()
-                a2(way, t, c).start()
-        for way in range(2):
-            b1_arrived(way, t).wait_recv()
-            b1(way, t + 1).start()
-            spread(-t - 1 if way == 0 else t + 1)
-        for c in (3, 2):
-            for way in range(2):
-                a2_arrived(way, t - 1, c).wait_recv()
-                a2(way, t, c).start()
-        forward(-t)
-        forward(t)
+                a2(way, t - 1, c, 1).wait_recv()
+                if way in ways:
+                    a2(way, t, c).start()
+        for o in (-t, t):
+            forward(o)
+            y_forward(o)
         if first:
+            y_share(0)
             finish(0)
             compute([0])
         else:
             finish(1 - t)
             finish(t - 1)
             compute([1 - t, t - 1])
-
-    turn(1, True)
+        y_share(-t)
+        y_share(t)
+
+    turn(1, first=True)
 
     @pl.loop(2, short - 1)
     def _(t):
-        turn(t, False)
-
-    t = short - 1
+        turn(t)
+
+    turn(short - 1, ahead=(True, False))
+    turn(long - 1, both=False, ahead=(False, False))
+    forward(-long)
+    y_forward(-long)
+    finish(1 - long)
+    finish(long - 1)
+    compute([1 - long, long - 1])
+    y_share(-long)
     for c in (0, 1, 3, 2):
-        for way in range(2):
-            a2_arrived(way, t - 1, c).wait_recv()
-            a2(way, t, c).start()
-        if c == 1:
-            b1_arrived(0, t).wait_recv()
-            b1(0, t + 1).start()
-            spread(-t - 1)
-            b1_arrived(1, t).wait_recv()
-            spread(t + 1)
-    forward(-t)
-    forward(t)
-    finish(1 - t)
-    finish(t - 1)
-    compute([1 - t, t - 1])
-    t = long - 1
-    for c in (0, 1, 3, 2):
-        a2_arrived(0, t - 1, c).wait_recv()
-        a2(0, t, c).start()
-        a2_arrived(1, t - 1, c).wait_recv()
-        if c == 1:
-            b1_arrived(0, t).wait_recv()
-            spread(-t - 1)
-    forward(-t)
-    forward(t)
-    finish(1 - t)
-    finish(t - 1)
-    compute([1 - t, t - 1])
-    forward(-long)
-    finish(-t)
-    finish(t)
-    compute([-t, t])
-    for c in (0, 1, 3, 2):
-        a2_arrived(0, t, c).wait_recv()
+        a2(0, long - 1, c, 1).wait_recv()
     finish(-long)
     compute([-long])
     out_ref[0] = acc[...].astype(BF16)
@@ -445,8 +549,12 @@
         remote(span, span, sem, ra1.at[0], to_z[0]).wait_send()
 
     sent(bufa, NX - 1, sa1.at[0])
-    sent(bufa, NX * long, sa2.at[0])
-    sent(bufa, NX * short, sa2.at[1])
+    sent(tokb.at[0], NX - 1, st1.at[0])
+    for way, count in ((0, long), (1, short)):
+        sent(bufa, NX * count, sa2.at[way])
+        sent(tokb.at[0], NX * count, st2.at[way])
+    sent(tokb, 3, sy.at[0])
+    sent(tokb, ny, ss.at[0])
     sent(bufb, long, sb1.at[0])
     sent(bufb, short, sb1.at[1])
     sent(bufb, 3 * nz, sb2.at[0])
@@ -455,6 +563,16 @@
     for j, p in zpeers:
         remote(send2.at[p], recv2.at[p], s2.at[p], r2.at[p], {"seq": x * nz + p}).wait_send()
 
+    @pl.when(me >= by_rows)
+    def _():
+        for t in range(ny - 1):
+            raw_to(t).wait_send()
+
+    @pl.when(me < by_rows)
+    def _():
+        for j, p in epeers:
+            rows_to(j, p).wait_send()
+
 
 def block(nz, ne, q, k, v, ld, sin, routes, gain, w_gate, w_up):
     tokens, width = q.shape
@@ -462,8 +580,9 @@
     rows = hd // nz
     _, hidden, depth = w_gate.shape
     units = NX * nz
-    ka = depth * 22 // 48 // 128 * 128
-    kb = depth + depth // 4 - ka
+    deep = depth - 2 * width
+    ka = 2 * width
+    kb = deep + deep // 4 - ka
     dma = pltpu.SemaphoreType.DMA
     vmem = pl.BlockSpec(memory_space=pltpu.VMEM)
     return pl.pallas_call(
@@ -494,8 +613,12 @@
             pltpu.VMEM((tokens, width), F32),
             pltpu.VMEM((ne, 32, width), BF16),
             pltpu.VMEM((ne, 32, width), BF16),
-            pltpu.VMEM((units, 16, ka), BF16),
+            pltpu.VMEM((ne, 1, hd), F32),
+            pltpu.VMEM((ne // 2, 16, width), BF16),
+            pltpu.VMEM((1, 16, width), BF16),
+            pltpu.VMEM((units, 16, ka + 128), BF16),
             pltpu.VMEM((units, 16, kb), BF16),
+            pltpu.VMEM((ne, units, 16, width), BF16),
             pltpu.VMEM((hidden, units * CAP), F32),
             dma((9,)),
             dma((nz,)),
@@ -508,14 +631,26 @@
             dma((nz,)),
             dma((ne,)),
             dma((ne,)),
+            dma((ne,)),
+            dma((ne,)),
+            dma((ne // 2,)),
+            dma((1,)),
             dma((1,)),
             dma((NX - 1,)),
+            dma((1,)),
+            dma((NX - 1,)),
+            dma((2,)),
+            dma((2, nz // 2, NX)),
             dma((2,)),
             dma((2, nz // 2, NX)),
             dma((2,)),
             dma((2, nz // 2)),
             dma((1,)),
             dma((3, 2 * nz)),
+            dma((1,)),
+            dma((3, 2 * nz)),
+            dma((1,)),
+            dma((2 * nz,)),
         ],
         compiler_params=pltpu.CompilerParams(
             collective_id=0, has_side_effects=True, vmem_limit_bytes=60 * 2**20

time: 152 us -> 149 us (0.980)
  Pallas kernels: 147 us -> 145 us
    pallas_call x1, Pallas kernels: 147 us -> 145 us  [block(): pl.pallas_call(functools.partial(block_kernel, nz, ne), out_shape=(jax.Sh...]
where the time goes in v3:
time: 149 us
  Pallas kernels  145 us (97%)
  local copies, waits for them, and re-layouts  3.03 us (2%)
    pallas_call x1, Pallas kernels, block(): pl.pallas_call(functools.partial(block_kernel, nz, ne), out_shape=(jax.Sh...  145 us
    unnamed x2, local copies, waits for them, and re-layouts  3.03 us

profile of v3, /device:TPU:1, one launch (start us, length us, event | category | flops | bytes accessed | tf_op | source)
XLA Modules:
  0.0 148.9 jit_solution(18018358640165713704)
XLA Ops:
  0.6 145.2 %shard_map.104 = (bf16[1,144,1280]{2,1,0:T(8,128)(2,1)}, f32[6,2,128]{2,1,0:T(2,128)}) custom-call(bf16[64,768]{1,0:T(8,128)(2,1)} %q_hbm.1, bf16[64,768]{1,0:T(8,128)(2,1)} %k_hbm.1, bf16[64,768]{1,0:T(8,128)(2,1)} %v_hbm.1, f32[6,64]{1,0:T(8,128)} %ld_hbm.1, f32[6,128,128]{2,1,0:T(8,128)} %sin_hbm.1, s32[2,64]{1,0:T(2,128)} %bitcast.3, f32[1,6144]{1,0:T(1,128)} %bitcast.2, ...), custom_call_target="tpu_custom_call" | custom-call | tf_op jit(solution)/shard_map/pallas_call | solution.py:588
  145.9 1.7 %copy.13 = bf16[1,144,1280]{2,1,0:T(8,128)(2,1)} copy(bf16[1,144,1280]{2,1,0:T(8,128)(2,1)} %get-tuple-element.4) | data formatting | bytes 737280
  147.6 1.3 copy.14

commit v4 on v3

--- a/solution.py
+++ b/solution.py
@@ -536,8 +536,8 @@
     y_forward(-long)
     finish(1 - long)
     finish(long - 1)
+    y_share(-long)
     compute([1 - long, long - 1])
-    y_share(-long)
     for c in (0, 1, 3, 2):
         a2(0, long - 1, c, 1).wait_recv()
     finish(-long)

time: 149 us -> 147 us (0.987)
  Pallas kernels: 145 us -> 143 us
    pallas_call x1, Pallas kernels: 145 us -> 143 us  [block(): pl.pallas_call(functools.partial(block_kernel, nz, ne), out_shape=(jax.Sh...]
where the time goes in v4:
time: 147 us
  Pallas kernels  143 us (97%)
  local copies, waits for them, and re-layouts  3.03 us (2%)
    pallas_call x1, Pallas kernels, block(): pl.pallas_call(functools.partial(block_kernel, nz, ne), out_shape=(jax.Sh...  143 us
    unnamed x2, local copies, waits for them, and re-layouts  3.03 us

profile of v4, /device:TPU:1, one launch (start us, length us, event | category | flops | bytes accessed | tf_op | source)
XLA Modules:
  0.0 147.0 jit_solution(10648196743069775865)
XLA Ops:
  0.6 143.4 %shard_map.104 = (bf16[1,144,1280]{2,1,0:T(8,128)(2,1)}, f32[6,2,128]{2,1,0:T(2,128)}) custom-call(bf16[64,768]{1,0:T(8,128)(2,1)} %q_hbm.1, bf16[64,768]{1,0:T(8,128)(2,1)} %k_hbm.1, bf16[64,768]{1,0:T(8,128)(2,1)} %v_hbm.1, f32[6,64]{1,0:T(8,128)} %ld_hbm.1, f32[6,128,128]{2,1,0:T(8,128)} %sin_hbm.1, s32[2,64]{1,0:T(2,128)} %bitcast.3, f32[1,6144]{1,0:T(1,128)} %bitcast.2, ...), custom_call_target="tpu_custom_call" | custom-call | tf_op jit(solution)/shard_map/pallas_call | solution.py:588
  144.0 1.7 %copy.13 = bf16[1,144,1280]{2,1,0:T(8,128)(2,1)} copy(bf16[1,144,1280]{2,1,0:T(8,128)(2,1)} %get-tuple-element.4) | data formatting | bytes 737280
  145.7 1.3 copy.14
